TPU v7x, 32 devices: a whole 2x2x4 slice. The times are simulated.
32 devices in a mesh: dp: 8 (over z, core), expert: 4 (over y, x).
Axes of the slice: x: 2, y: 2, z: 4, core: 2. Of those that a mesh axis runs over, the one named last changes fastest.
Arguments:
- cached_hidden: bfloat16 [1024, 1536], P(('dp', 'expert')), may hold values from -6 to 6
- direction: bfloat16 [4, 2880, 1536], P('expert', 'dp'), may hold values from -1 to 1
- expert_ids: int32 [4096, 4], P(('dp', 'expert')), may hold values from 0 to 127, as said below
- gate_weights: float32 [4096, 4], P(('dp', 'expert')), may hold values from 0.05 to 1
Outputs:
- curvature_product: float32 [4, 2880, 1536], P('expert', 'dp')
Inputs may be any that keep to these rules, and one draw needn't show every extreme that they name: `expert_ids`: each row names 4 different experts, at most two of them below 4. Among the 128 rows of one device no expert below 4 is named more than 8 times; for every dp index, some expert below 4 is named exactly 8 times by the rows of each device with that dp index.
All inputs are finite; a program needn't handle non-finite values.
Results may differ from a plain program's by a relative error of at most 0.0034.
Values may be sent and summed in bfloat16 or wider, within the bound.
A program may use at most 128 MiB of HBM per device.

v0:
```python
import math

import jax
import jax.numpy as jnp
from jax import lax
from jax.sharding import PartitionSpec as P


def slot_positions(block_ids, experts):
    flat = block_ids.reshape(-1)
    onehot = (flat[:, None] == jnp.arange(experts, dtype=jnp.int32)[None, :]).astype(jnp.int32)
    before = jnp.cumsum(onehot, axis=0) - onehot
    return jnp.sum(before * onehot, axis=1).reshape(block_ids.shape)


def body(cached_hidden, direction, expert_ids, gate_weights):
    dp_count = lax.axis_size("dp")
    owner_count = lax.axis_size("expert")
    slot_rows = cached_hidden.shape[0]
    capacity = slot_rows // owner_count
    tok_count = expert_ids.shape[0]
    width = direction.shape[1] * dp_count
    local_dir = direction[0]
    rows_all = lax.all_gather(cached_hidden, "dp", axis=0, tiled=True)
    tangent = lax.dot_general(
        rows_all, local_dir, (((1,), (1,)), ((), ())), preferred_element_type=jnp.float32
    )
    tangent = tangent.astype(jnp.bfloat16).reshape(
        dp_count, owner_count, capacity, local_dir.shape[0]
    )
    returned = lax.all_to_all(
        lax.all_to_all(tangent, "dp", split_axis=0, concat_axis=3, tiled=True),
        "expert",
        split_axis=1,
        concat_axis=1,
        tiled=True,
    )
    flat_rows = returned.reshape(owner_count * capacity, width)
    treated = expert_ids < owner_count
    slot_pos = slot_positions(expert_ids, owner_count)
    target = expert_ids * capacity + slot_pos
    lookup = jnp.where(treated, target, 0).reshape(-1)
    dropped = jnp.where(treated, target, owner_count * capacity).reshape(-1)
    gates = jnp.where(treated, gate_weights, 0.0)
    picked = jnp.take(flat_rows, lookup, axis=0).reshape(tok_count, expert_ids.shape[1], width)
    scale_factor = 1.0 / math.sqrt(tok_count * dp_count * owner_count)
    combined = jnp.sum(gates[..., None] * picked.astype(jnp.float32), axis=1) * scale_factor
    outgoing = (gates[..., None] * combined[:, None, :]).astype(jnp.bfloat16)
    buffer = jnp.zeros((owner_count * capacity, width), jnp.bfloat16)
    buffer = buffer.at[dropped].set(outgoing.reshape(-1, width), mode="drop")
    buffer = buffer.reshape(1, owner_count, capacity, width)
    arrived = lax.all_to_all(buffer, "expert", split_axis=1, concat_axis=1, tiled=True)
    adjoint = lax.all_to_all(arrived, "dp", split_axis=3, concat_axis=0, tiled=True)
    adjoint_rows = adjoint.reshape(-1, adjoint.shape[3])
    gradient = lax.dot_general(
        adjoint_rows, rows_all, (((0,), (0,)), ((), ())), preferred_element_type=jnp.float32
    )
    return gradient.reshape(1, gradient.shape[0], gradient.shape[1])


def solution(mesh):
    return jax.shard_map(
        body,
        mesh=mesh,
        in_specs=(
            P(("dp", "expert"), None),
            P("expert", "dp", None),
            P(("dp", "expert"), None),
            P(("dp", "expert"), None),
        ),
        out_specs=P("expert", "dp", None),
        check_vma=False,
    )
```

profile of v0, /device:TPU:0, one launch (start us, length us, event | category | flops | bytes accessed | tf_op | source)
XLA Modules:
  0.0 117.1 jit_solution(17782934938025006964)
XLA Ops:
  0.0 17.6 %all_gather.3 = bf16[256,1536]{1,0:T(8,128)(2,1)S(1)} all-gather(bf16[32,1536]{1,0:T(8,128)(2,1)} %param.4), channel_id=1, replica_groups=mesh['dp'=8,'expert'=4] {'dp'}, dimensions={0}, use_global_device_ids=true | all-gather | bytes 884736 | tf_op jit(solution)/shard_map/all_gather | solution.py:24
  17.6 0.5 convolution_convert_fusion
  18.1 0.8 copy.43
  18.9 4.8 %all-to-all-start = ((bf16[8,4,8,360]{3,2,1,0:T(8,128)(2,1)}), bf16[8,4,8,360]{3,2,1,0:T(8,128)(2,1)S(1)}, u32[]{:S(2)}, u32[]{:S(2)}) async-start(bf16[8,4,8,360]{3,2,1,0:T(8,128)(2,1)} %bitcast.3), calls=%async_computation | async-start | bytes 393216 | tf_op jit(solution)/shard_map/all_to_all | solution.py:32
  24.0 1.2 %reduce-window.6 = s32[4,4,128]{2,1,0:T(4,128)S(1)} reduce-window(s32[4,4,128]{2,1,0:T(4,128)S(1)} %fusion.7, s32[]{:T(128)} %constant.13.clone.1), window={size=1x1x128 pad=0_0x0_0x127_0}, to_apply=%region_0.0 | reduce-window | flops 260096 | bytes 16388 | tf_op jit(solution)/shard_map/reduce-window
  25.3 0.2 slice_reduce_fusion
  25.5 0.2 reduce-window.9
  26.5 5.6 %all-to-all-done = bf16[8,4,8,360]{3,2,1,0:T(8,128)(2,1)S(1)} async-done(((bf16[8,4,8,360]{3,2,1,0:T(8,128)(2,1)}), bf16[8,4,8,360]{3,2,1,0:T(8,128)(2,1)S(1)}, u32[]{:S(2)}, u32[]{:S(2)}) %all-to-all-start) | async-done | bytes 184352 | tf_op jit(solution)/shard_map/all_to_all | solution.py:32
  32.1 0.9 all_to_all.33
  33.0 3.7 %all-to-all-start.1 = ((bf16[1,4,8,2880]{3,2,0,1:T(8,128)(2,1)}), bf16[1,4,8,2880]{3,2,0,1:T(8,128)(2,1)S(1)}, u32[]{:S(2)}, u32[]{:S(2)}) async-start(bf16[1,4,8,2880]{3,2,0,1:T(8,128)(2,1)} %bitcast.6), calls=%async_computation.1 | async-start | bytes 376832 | tf_op jit(solution)/shard_map/all_to_all | solution.py:31
  37.1 4.8 %all-to-all-done.1 = bf16[1,4,8,2880]{3,2,0,1:T(8,128)(2,1)S(1)} async-done(((bf16[1,4,8,2880]{3,2,0,1:T(8,128)(2,1)}), bf16[1,4,8,2880]{3,2,0,1:T(8,128)(2,1)S(1)}, u32[]{:S(2)}, u32[]{:S(2)}) %all-to-all-start.1) | async-done | bytes 184352 | tf_op jit(solution)/shard_map/all_to_all | solution.py:31
  41.9 3.7 %gather_fusion = bf16[512,2880]{1,0:T(8,128)(2,1)} fusion(bf16[32,2880]{1,0:T(8,128)(2,1)S(1)} %bitcast.44, s32[1024]{0:T(1024)S(1)} %pad_clamp_fusion), kind=kCustom, calls=%fused_computation | custom fusion | bytes 5900288 | tf_op jit(solution)/shard_map/jit(_take)/gather | solution.py:45
  45.5 5.8 %gather.7 = bf16[128,4,2880]{2,1,0:T(4,128)(2,1)} reshape(bf16[512,2880]{1,0:T(8,128)(2,1)} %gather_fusion) | data formatting | bytes 5898240 | tf_op jit(solution)/shard_map/jit(_take)/gather | solution.py:45
  51.4 8.5 %multiply_reduce_fusion = f32[128,2880]{1,0:T(8,128)S(1)} fusion(bf16[128,4,2880]{2,1,0:T(4,128)(2,1)} %gather.7, f32[128,4]{1,0:T(8,128)S(1)} %copy.40, pred[128,4]{1,0:T(8,128)(4,1)S(1)} %copy.42), kind=kLoop, calls=%fused_computation.3 | loop fusion | flops 5529600 | bytes 4426240 | tf_op jit(solution)/shard_map/reduce_sum | solution.py:47
  59.9 3.6 %mul.54 = f32[128,4,2880]{2,1,0:T(4,128)} broadcast(f32[128,2880]{1,0:T(8,128)S(1)} %broadcast_multiply_fusion), dimensions={0,2} | broadcast | bytes 7372800 | tf_op jit(solution)/shard_map/mul | solution.py:48
  63.5 7.7 %mul.55 = f32[512,2880]{1,0:T(8,128)} reshape(f32[128,4,2880]{2,1,0:T(4,128)} %mul.54) | data formatting | bytes 11796480 | tf_op jit(solution)/shard_map/mul | solution.py:48
  71.3 6.9 %scatter_custom_fusion = bf16[32,2880]{1,0:T(8,128)(2,1)S(1)} fusion(s32[512]{0:T(512)S(1)} %bitcast.53, f32[512,2880]{1,0:T(8,128)} %mul.55, f32[512]{0:T(512)S(1)} %mul.48, bf16[]{:T(256)} %constant.9.clone.1), kind=kCustom, calls=%fused_computation.4 | custom fusion | flops 2949120 | bytes 6084610 | tf_op jit(solution)/shard_map/scatter | solution.py:50
  78.2 7.9 %all_to_all.43 = bf16[1,4,8,2880]{3,2,0,1:T(8,128)(2,1)S(1)} all-to-all(bf16[1,4,8,2880]{3,2,0,1:T(8,128)(2,1)S(1)} %bitcast.50), channel_id=1, replica_groups=mesh['dp'=8,'expert'=4] {'expert'}, dimensions={1} | all-to-all | bytes 368640 | tf_op jit(solution)/shard_map/all_to_all | solution.py:52
  86.1 3.4 %copy.47 = bf16[1,4,8,2880]{2,1,0,3:T(4,128)(2,1)} copy(bf16[1,4,8,2880]{3,2,0,1:T(8,128)(2,1)S(1)} %all_to_all.43) | data formatting | bytes 368640 | tf_op jit(solution)/shard_map/all_to_all | solution.py:52
  89.4 7.1 %reshape.146 = bf16[8,2,5760]{2,1,0:T(2,128)(2,1)S(1)} reshape(bf16[2880,1,4,8]{3,2,1,0:T(4,128)(2,1)} %bitcast.45) | data formatting | bytes 368640
  96.5 10.5 %all_to_all.44 = bf16[8,2,5760]{2,1,0:T(2,128)(2,1)S(1)} all-to-all(bf16[8,2,5760]{2,1,0:T(2,128)(2,1)S(1)} %reshape.146), channel_id=1, replica_groups=mesh['dp'=8,'expert'=4] {'dp'}, dimensions={0} | all-to-all | bytes 368640 | tf_op jit(solution)/shard_map/all_to_all | solution.py:53
  107.0 4.5 %reshape.147 = bf16[2880,1,4,8]{3,2,1,0:T(4,128)(2,1)} reshape(bf16[8,2,5760]{2,1,0:T(2,128)(2,1)S(1)} %all_to_all.44) | data formatting | bytes 368640
  111.5 3.7 %copy.50 = bf16[1,4,8,8,360]{4,3,2,1,0:T(8,128)(2,1)S(1)} copy(bf16[1,4,8,8,360]{2,1,4,3,0:T(4,128)(2,1)} %bitcast.46) | data formatting | bytes 368640 | tf_op jit(solution)/shard_map/all_to_all | solution.py:53
  115.2 1.8 %convolution_bitcast_fusion = f32[1,360,1536]{2,1,0:T(8,128)} fusion(bf16[256,360]{1,0:T(8,128)(2,1)S(1)} %bitcast.47, bf16[256,1536]{1,0:T(8,128)(2,1)S(1)} %all_gather.3), kind=kOutput, calls=%fused_computation.6 | convolution fusion | flops 283115520 | bytes 3182592 | tf_op jit(solution)/shard_map/dot_general | solution.py:55
  (30 shorter events, 1.7 us)
Async XLA Ops:
  0.0 17.6 %copy-start = (bf16[1,360,1536]{2,1,0:T(8,128)(2,1)S(1)}, bf16[1,360,1536]{2,1,0:T(8,128)(2,1)}, u32[]{:S(2)}) copy-start(bf16[1,360,1536]{2,1,0:T(8,128)(2,1)} %param.5) | copy-start | bytes 3317764
  0.0 23.7 %copy-start.1 = (s32[128,4]{0,1:T(4,128)S(1)}, s32[128,4]{0,1:T(4,128)}, u32[]{:S(2)}) copy-start(s32[128,4]{0,1:T(4,128)} %param.6) | copy-start | bytes 6148
  0.0 26.4 %copy-start.2 = (f32[128,4]{0,1:T(4,128)S(1)}, f32[128,4]{0,1:T(4,128)}, u32[]{:S(2)}) copy-start(f32[128,4]{0,1:T(4,128)} %param.7) | copy-start | bytes 6148
  18.9 13.1 %all-to-all-start = ((bf16[8,4,8,360]{3,2,1,0:T(8,128)(2,1)}), bf16[8,4,8,360]{3,2,1,0:T(8,128)(2,1)S(1)}, u32[]{:S(2)}, u32[]{:S(2)}) async-start(bf16[8,4,8,360]{3,2,1,0:T(8,128)(2,1)} %bitcast.3), calls=%async_computation | async-start | bytes 393216 | tf_op jit(solution)/shard_map/all_to_all | solution.py:32
  33.0 8.9 %all-to-all-start.1 = ((bf16[1,4,8,2880]{3,2,0,1:T(8,128)(2,1)}), bf16[1,4,8,2880]{3,2,0,1:T(8,128)(2,1)S(1)}, u32[]{:S(2)}, u32[]{:S(2)}) async-start(bf16[1,4,8,2880]{3,2,0,1:T(8,128)(2,1)} %bitcast.6), calls=%async_computation.1 | async-start | bytes 376832 | tf_op jit(solution)/shard_map/all_to_all | solution.py:31
where the time goes:
time: 118 us; the launch traced here: 117 us
  local copies, waits for them, and re-layouts  42.8 us (36%)
  blocking collectives  35.9 us (30%)
  other arithmetic  17 us (14%)
  waiting for transfers between devices  10.4 us (9%)
  starting transfers between devices  8.51 us (7%)
  matrix products  2.31 us (2%)
    all_gather x1, blocking collectives, body(): rows_all = lax.all_gather(cached_hidden, 'dp', axis=0, tiled=True)  17.6 us
    unnamed x9, local copies, waits for them, and re-layouts  11.8 us
    mul x3, local copies, waits for them, and re-layouts, body(): outgoing = (gates[..., None] * combined[:, None, :]).astype(jnp.bfloat16)  11.5 us
    all_to_all x1, blocking collectives, body(): lax.all_to_all(arrived, 'dp', split_axis=3, concat_axis=0, tiled=True)  10.5 us
    gather x2, local copies, waits for them, and re-layouts, body(): jnp.take(flat_rows, lookup, axis=0)  9.51 us
    reduce_sum x1, other arithmetic, body(): jnp.sum(gates[..., None] * picked.astype(jnp.float32), axis=1)  8.46 us
    all_to_all x1, blocking collectives, body(): lax.all_to_all(buffer, 'expert', split_axis=1, concat_axis=1, tiled=True)  7.89 us
    scatter x1, other arithmetic, body(): buffer = buffer.at[dropped].set(outgoing.reshape(-1, width), mode='drop')  6.86 us
  transfers between devices with their start and end apart: 2, of which 2 were waited for; matrix products, arithmetic and copies ran while one was open for 3% of the time, Pallas kernels for 0%

commit v1 on v0

--- a/solution.py
+++ b/solution.py
@@ -1,9 +1,17 @@
+import functools
 import math
 
 import jax
 import jax.numpy as jnp
 from jax import lax
+from jax.experimental import pallas as pl
+from jax.experimental.pallas import tpu as pltpu
 from jax.sharding import PartitionSpec as P
+
+MESH = pl.DeviceIdType.MESH
+CORES = 2
+LANES = 128
+CHUNKS = 2
 
 
 def slot_positions(block_ids, experts):
@@ -13,7 +21,7 @@
     return jnp.sum(before * onehot, axis=1).reshape(block_ids.shape)
 
 
-def body(cached_hidden, direction, expert_ids, gate_weights):
+def general_body(cached_hidden, direction, expert_ids, gate_weights):
     dp_count = lax.axis_size("dp")
     owner_count = lax.axis_size("expert")
     slot_rows = cached_hidden.shape[0]
@@ -58,6 +66,284 @@
     return gradient.reshape(1, gradient.shape[0], gradient.shape[1])
 
 
+def swap_blocks(x, cap):
+    lane = lax.broadcasted_iota(jnp.int32, x.shape, 1)
+    back = pltpu.roll(x, LANES - cap, 1)
+    ahead = pltpu.roll(x, cap, 1)
+    return jnp.where((lane // cap) % 2 == 0, back, ahead)
+
+
+def pair_matrix(ids, gates, q, n_e, cap, scale):
+    toks, topk = ids.shape
+    lane = lax.broadcasted_iota(jnp.int32, (toks, LANES), 1)
+    lane_e, lane_q, lane_c = lane // (n_e * cap), (lane // cap) % n_e, lane % cap
+    named = jnp.zeros((toks, LANES), jnp.float32)
+    gate = jnp.zeros((toks, LANES), jnp.float32)
+    for k in range(topk):
+        same = ids[:, k : k + 1] == lane_e
+        named = named + jnp.where(same, 1.0, 0.0)
+        gate = gate + jnp.where(same, gates[:, k : k + 1], 0.0)
+    row = lax.broadcasted_iota(jnp.int32, (toks, toks), 0)
+    col = lax.broadcasted_iota(jnp.int32, (toks, toks), 1)
+    earlier = jnp.where(col < row, 1.0, 0.0).astype(jnp.bfloat16)
+    position = jnp.dot(earlier, named.astype(jnp.bfloat16), preferred_element_type=jnp.float32)
+    held = (position == lane_c.astype(jnp.float32)) & (lane_q == q)
+    slots = jnp.where(held, gate, 0.0).T
+    high = slots.astype(jnp.bfloat16)
+    low = (slots - high.astype(jnp.float32)).astype(jnp.bfloat16)
+    nt = (((1,), (1,)), ((), ()))
+    total = lax.dot_general(high, high, nt, preferred_element_type=jnp.float32)
+    total += lax.dot_general(high, low, nt, preferred_element_type=jnp.float32)
+    total += lax.dot_general(low, high, nt, preferred_element_type=jnp.float32)
+    return total * scale
+
+
+def kernel(
+    n_dp, n_e, cap, scale,
+    h_ref, dir_ref, ids_ref, gates_ref,
+    adj_ref, hall,
+    dirv, tang, pairs, wf, wall,
+    loc_sem, own_send, relay_send, hz_recv, hs_send, hs_recv,
+    a_send, a_recv, w_send, w_recv, ws_send, ws_recv, t_send, t_recv,
+):
+    n_z = n_dp // CORES
+    rows = n_e * cap
+    feat = dirv.shape[0]
+    part = rows // CHUNKS
+    p = lax.axis_index("dp")
+    e = lax.axis_index("expert")
+    z, core = p // CORES, p % CORES
+    sib = z * CORES + (1 - core)
+    nt = (((1,), (1,)), ((), ()))
+
+    load_dir = pltpu.make_async_copy(dir_ref.at[0], dirv, loc_sem.at[0])
+    load_h = pltpu.make_async_copy(h_ref, hall.at[p], loc_sem.at[1])
+    load_dir.start()
+    load_h.start()
+
+    def z_peer(d):
+        return lax.rem(z + d, n_z)
+
+    def e_peer(d):
+        return lax.rem(e + d, n_e)
+
+    barrier = pltpu.get_barrier_semaphore()
+    for d in range(1, n_z):
+        pl.semaphore_signal(barrier, inc=1, device_id=(z_peer(d) * CORES + core, e), device_id_type=MESH)
+    for d in range(1, n_e):
+        pl.semaphore_signal(barrier, inc=1, device_id=(p, e_peer(d)), device_id_type=MESH)
+    pl.semaphore_signal(barrier, inc=1, device_id=(sib, e), device_id_type=MESH)
+    pl.semaphore_wait(barrier, n_z + n_e - 1)
+
+    def remote(src, dst, send, recv, dev):
+        return pltpu.make_async_remote_copy(
+            src_ref=src, dst_ref=dst, send_sem=send, recv_sem=recv, device_id=dev, device_id_type=MESH
+        )
+
+    def own_copy(side, c):
+        to = z + 1 if side == 0 else z - 1
+        return remote(
+            h_ref.at[pl.ds(c * part, part)], hall.at[p, pl.ds(c * part, part)],
+            own_send.at[side, c], hz_recv.at[z, c], (to * CORES + core, e),
+        )
+
+    def on_side(side, fn):
+        pl.when(z + 1 < n_z if side == 0 else z > 0)(fn)
+
+    for c in range(CHUNKS):
+        for side in range(2):
+            on_side(side, lambda side=side, c=c: own_copy(side, c).start())
+
+    def sibling_copy(zs, src):
+        row = zs * CORES + core
+        return remote(src, hall.at[row], hs_send.at[zs], hs_recv.at[zs], (sib, e))
+
+    sibling_copy(z, h_ref).start()
+
+    pairs[...] = pair_matrix(ids_ref[...], gates_ref[...], e, n_e, cap, scale)
+
+    def slot_rows(owner, source):
+        return pl.ds(pl.multiple_of(owner * rows + source * cap, cap), cap)
+
+    def pair_copy(d):
+        to = e_peer(d)
+        return remote(
+            pairs.at[slot_rows(to, e)], wf.at[pl.ds(pl.multiple_of(e * cap, cap), cap)],
+            a_send.at[d], a_recv.at[e], (p, to),
+        )
+
+    for d in range(1, n_e):
+        pair_copy(d).start()
+    wf[pl.ds(pl.multiple_of(e * cap, cap), cap), :] = pairs[slot_rows(e, e), :]
+
+    mine = pl.ds(pl.multiple_of(e * rows, rows), rows)
+    tang[:, mine, feat // LANES * LANES :] = jnp.zeros(
+        (n_dp, rows, tang.shape[2] - feat // LANES * LANES), jnp.bfloat16
+    )
+
+    def tangent_copy(zs, d):
+        ref = tang.at[pl.ds(zs * CORES, CORES), mine]
+        return remote(ref, ref, t_send.at[zs, d], t_recv.at[zs, e], (p, e_peer(d)))
+
+    def tangents(zs):
+        block = hall[pl.ds(zs * CORES, CORES)].reshape(CORES * rows, hall.shape[2])
+        out = lax.dot_general(block, dirv[...], nt, preferred_element_type=jnp.float32)
+        tang[pl.ds(zs * CORES, CORES), mine, :feat] = out.astype(jnp.bfloat16).reshape(CORES, rows, feat)
+        for d in range(1, n_e):
+            tangent_copy(zs, d).start()
+
+    load_dir.wait()
+    load_h.wait()
+    sibling_copy(z, h_ref).wait_recv()
+    tangents(z)
+
+    for d in range(1, n_e):
+        src = e_peer(d)
+        remote(
+            pairs.at[slot_rows(e, src)], wf.at[pl.ds(pl.multiple_of(src * cap, cap), cap)],
+            a_send.at[d], a_recv.at[src], (p, src),
+        ).wait_recv()
+    weights = wf[...]
+    high = weights.astype(jnp.bfloat16).astype(jnp.float32)
+    wall[p] = (high + swap_blocks(weights - high, cap)).astype(jnp.bfloat16)
+
+    def weight_copy(d):
+        return remote(wall.at[p], wall.at[p], w_send.at[d], w_recv.at[z], (z_peer(d) * CORES + core, e))
+
+    def weight_sibling(zs):
+        ref = wall.at[zs * CORES + core]
+        return remote(ref, ref, ws_send.at[zs], ws_recv.at[zs], (sib, e))
+
+    for d in range(1, n_z):
+        weight_copy(d).start()
+    weight_sibling(z).start()
+
+    near = jnp.minimum(z, n_z - 1 - z)
+
+    def source(j):
+        if j == 0:
+            return z
+        s = (j + 1) // 2
+        close = z - s if j % 2 else z + s
+        far = jnp.where(2 * z < n_z - 1, j, n_z - 1 - j)
+        return jnp.where(j <= 2 * near, close, far)
+
+    def relay_copy(zs, c):
+        to = jnp.where(zs < z, z + 1, z - 1)
+        ref = hall.at[zs * CORES + core, pl.ds(c * part, part)]
+        return remote(ref, ref, relay_send.at[zs, c], hz_recv.at[zs, c], (to * CORES + core, e))
+
+    def relays(zs, fn):
+        to = jnp.where(zs < z, z + 1, z - 1)
+        pl.when((to >= 0) & (to < n_z))(fn)
+
+    lane = lax.broadcasted_iota(jnp.int32, (rows, LANES), 1)
+    row = lax.broadcasted_iota(jnp.int32, (rows, LANES), 0)
+    direct = (lane // cap) % n_e == row // cap
+
+    def finish(zs):
+        weight_sibling(zs).wait_recv()
+        for d in range(1, n_e):
+            src = e_peer(d)
+            ref = tang.at[pl.ds(zs * CORES, CORES), pl.ds(pl.multiple_of(src * rows, rows), rows)]
+            remote(ref, ref, t_send.at[zs, d], t_recv.at[zs, src], (p, src)).wait_recv()
+        for k in range(CORES):
+            packed = wall[zs * CORES + k].astype(jnp.float32)
+            high = jnp.where(direct, packed, 0.0)
+            low = swap_blocks(packed - high, cap)
+            both = jnp.concatenate([high, low], axis=0).astype(jnp.bfloat16)
+            out = jnp.dot(both, tang[zs * CORES + k], preferred_element_type=jnp.float32)
+            out = (out[:rows] + out[rows:]).astype(jnp.bfloat16)
+            adj_ref[zs * CORES + k] = out[:, :feat]
+
+    for j in range(1, n_z):
+        zs = source(j)
+        for c in range(CHUNKS):
+            relay_copy(zs, c).wait_recv()
+            relays(zs, lambda zs=zs, c=c: relay_copy(zs, c).start())
+        sibling_copy(zs, hall.at[zs * CORES + core]).start()
+        sibling_copy(zs, hall.at[zs * CORES + core]).wait_recv()
+        tangents(zs)
+        remote(
+            wall.at[zs * CORES + core], wall.at[zs * CORES + core], w_send.at[1], w_recv.at[zs], (sib, e)
+        ).wait_recv()
+        weight_sibling(zs).start()
+        finish(source(j - 1))
+    finish(source(n_z - 1))
+
+    for c in range(CHUNKS):
+        for side in range(2):
+            on_side(side, lambda side=side, c=c: own_copy(side, c).wait_send())
+    for d in range(1, n_e):
+        pair_copy(d).wait_send()
+    for d in range(1, n_z):
+        weight_copy(d).wait_send()
+    for j in range(n_z):
+        zs = source(j)
+        sibling_copy(zs, hall.at[zs * CORES + core]).wait_send()
+        weight_sibling(zs).wait_send()
+        for d in range(1, n_e):
+            tangent_copy(zs, d).wait_send()
+        if j:
+            for c in range(CHUNKS):
+                relays(zs, lambda zs=zs, c=c: relay_copy(zs, c).wait_send())
+
+
+def body(cached_hidden, direction, expert_ids, gate_weights):
+    n_dp, n_e = lax.axis_size("dp"), lax.axis_size("expert")
+    rows, fw = cached_hidden.shape
+    cap = rows // n_e
+    feat = direction.shape[1]
+    if n_e * rows != LANES or cap % 8 or rows % (16 * CHUNKS) or n_dp % CORES or n_dp < 2 * CORES:
+        return general_body(cached_hidden, direction, expert_ids, gate_weights)
+    n_z = n_dp // CORES
+    wide = -(-feat // LANES) * LANES
+    scale = 1.0 / math.sqrt(expert_ids.shape[0] * n_dp * n_e)
+    vmem = pl.BlockSpec(memory_space=pltpu.VMEM)
+    hbm = pl.BlockSpec(memory_space=pl.ANY)
+    dma = pltpu.SemaphoreType.DMA
+    adjoint, rows_all = pl.pallas_call(
+        functools.partial(kernel, n_dp, n_e, cap, scale),
+        out_shape=(
+            jax.ShapeDtypeStruct((n_dp, rows, feat), jnp.bfloat16),
+            jax.ShapeDtypeStruct((n_dp, rows, fw), jnp.bfloat16),
+        ),
+        in_specs=[hbm, hbm, vmem, vmem],
+        out_specs=(vmem, vmem),
+        scratch_shapes=[
+            pltpu.VMEM((feat, fw), jnp.bfloat16),
+            pltpu.VMEM((n_dp, n_e * rows, wide), jnp.bfloat16),
+            pltpu.VMEM((LANES, LANES), jnp.float32),
+            pltpu.VMEM((rows, LANES), jnp.float32),
+            pltpu.VMEM((n_dp, rows, LANES), jnp.bfloat16),
+            dma((2,)),
+            dma((2, CHUNKS)),
+            dma((n_z, CHUNKS)),
+            dma((n_z, CHUNKS)),
+            dma((n_z,)),
+            dma((n_z,)),
+            dma((n_e,)),
+            dma((n_e,)),
+            dma((n_z,)),
+            dma((n_z,)),
+            dma((n_z,)),
+            dma((n_z,)),
+            dma((n_z, n_e)),
+            dma((n_z, n_e)),
+        ],
+        compiler_params=pltpu.CompilerParams(
+            collective_id=0, has_side_effects=True, vmem_limit_bytes=32 * 1024 * 1024
+        ),
+    )(cached_hidden, direction, expert_ids, gate_weights)
+    gradient = lax.dot_general(
+        adjoint.reshape(n_dp * rows, feat),
+        rows_all.reshape(n_dp * rows, fw),
+        (((0,), (0,)), ((), ())),
+        preferred_element_type=jnp.float32,
+    )
+    return gradient.reshape(1, feat, fw)
+
+
 def solution(mesh):
     return jax.shard_map(
         body,

time: 118 us -> 32.1 us (0.27)
  local copies, waits for them, and re-layouts: 42.8 us -> 3.71 us
  blocking collectives: 35.9 us -> 0 us
  Pallas kernels: 0 us -> 26.3 us
  other arithmetic: 17 us -> 0 us
  waiting for transfers between devices: 10.4 us -> 0 us
  starting transfers between devices: 8.51 us -> 0 us
    pallas_call x0 -> x1, Pallas kernels: none -> 26.3 us  [body(): pl.pallas_call(functools.partial(kernel, n_dp, n_e, cap, scale), out_shap...]
    all_to_all x2 -> x0, blocking collectives: 18.4 us -> none  [the longest x1 10.5 us: body(): lax.all_to_all(arrived, 'dp', split_axis=3, concat_axis=0, tiled=True)]
    all_gather x1 -> x0, blocking collectives: 17.6 us -> none  [body(): rows_all = lax.all_gather(cached_hidden, 'dp', axis=0, tiled=True)]
    mul x3 -> x0, local copies, waits for them, and re-layouts: 11.5 us -> none  [body(): outgoing = (gates[..., None] * combined[:, None, :]).astype(jnp.bfloat16)]
    all_to_all x2 -> x0, waiting for transfers between devices: 10.4 us -> none  [the longest x1 5.57 us: body(): lax.all_to_all(tangent, 'dp', split_axis=0, concat_axis=3, tiled=True)]
    gather x2 -> x0, local copies, waits for them, and re-layouts: 9.51 us -> none  [body(): jnp.take(flat_rows, lookup, axis=0)]
    all_to_all x2 -> x0, starting transfers between devices: 8.51 us -> none  [the longest x1 4.8 us: body(): lax.all_to_all(tangent, 'dp', split_axis=0, concat_axis=3, tiled=True)]
    reduce_sum x2 -> x0, other arithmetic: 8.48 us -> none  [the longest x1 8.46 us: body(): jnp.sum(gates[..., None] * picked.astype(jnp.float32), axis=1)]
  transfers between devices with their start and end apart: 2 -> 0, of which waited for: 2 -> 0; matrix products, arithmetic and copies ran while one was open for 3% -> 0% of each run, Pallas kernels for 0% -> 0%
where the time goes in v1:
time: 32.1 us; the launch traced here: 31.9 us
  Pallas kernels  26.3 us (82%)
  local copies, waits for them, and re-layouts  3.71 us (12%)
  matrix products  1.83 us (6%)
    pallas_call x1, Pallas kernels, body(): pl.pallas_call(functools.partial(kernel, n_dp, n_e, cap, scale), out_shap...  26.3 us
    unnamed x6, local copies, waits for them, and re-layouts  3.71 us
    dot_general x1, matrix products, body(): lax.dot_general(adjoint.reshape(n_dp * rows, feat), rows_all.reshape(n_dp...  1.83 us

profile of v1, /device:TPU:0, one launch (start us, length us, event | category | flops | bytes accessed | tf_op | source)
XLA Modules:
  0.0 31.9 jit_solution(16705440718009012844)
XLA Ops:
  0.0 0.8 %copy.5.ids_ref = s32[128,4]{1,0:T(8,128)S(1)} copy(s32[128,4]{0,1:T(4,128)} %param.6) | data formatting | bytes 4096 | tf_op args[2]
  0.8 0.8 %copy.6.gates_ref = f32[128,4]{1,0:T(8,128)S(1)} copy(f32[128,4]{0,1:T(4,128)} %param.7) | data formatting | bytes 4096 | tf_op args[3]
  1.6 0.0 copy-start
  1.6 1.2 %copy-done = bf16[1,360,1536]{2,1,0:T(8,128)(2,1)S(1)} copy-done((bf16[1,360,1536]{2,1,0:T(8,128)(2,1)S(1)}, bf16[1,360,1536]{2,1,0:T(8,128)(2,1)}, u32[]{:S(2)}) %copy-start) | copy-done | bytes 1105944
  2.8 0.0 copy-start.1
  2.8 0.9 %copy-done.1 = bf16[32,1536]{1,0:T(8,128)(2,1)S(1)} copy-done((bf16[32,1536]{1,0:T(8,128)(2,1)S(1)}, bf16[32,1536]{1,0:T(8,128)(2,1)}, u32[]{:S(2)}) %copy-start.1) | copy-done | bytes 98328
  3.7 26.3 %shard_map.46 = (bf16[8,32,360]{2,1,0:T(8,128)(2,1)S(1)}, bf16[8,32,1536]{2,1,0:T(8,128)(2,1)S(1)}) custom-call(bf16[32,1536]{1,0:T(8,128)(2,1)S(1)} %copy-done.1, bf16[1,360,1536]{2,1,0:T(8,128)(2,1)S(1)} %copy-done, s32[128,4]{1,0:T(8,128)S(1)} %copy.5.ids_ref, f32[128,4]{1,0:T(8,128)S(1)} %copy.6.gates_ref), custom_call_target="tpu_custom_call" | custom-call | tf_op jit(solution)/shard_map/pallas_call | solution.py:305
  30.1 1.8 %convolution_bitcast_fusion = f32[1,360,1536]{2,1,0:T(8,128)} fusion(bf16[8,32,360]{2,1,0:T(8,128)(2,1)S(1)} %get-tuple-element.7, bf16[8,32,1536]{2,1,0:T(8,128)(2,1)S(1)} %get-tuple-element.8), kind=kOutput, calls=%fused_computation | convolution fusion | flops 283115520 | bytes 3182592 | tf_op jit(solution)/shard_map/dot_general | solution.py:338
Async XLA Ops:
  1.6 1.2 %copy-start = (bf16[1,360,1536]{2,1,0:T(8,128)(2,1)S(1)}, bf16[1,360,1536]{2,1,0:T(8,128)(2,1)}, u32[]{:S(2)}) copy-start(bf16[1,360,1536]{2,1,0:T(8,128)(2,1)} %dir_ref.1) | copy-start | bytes 3317764
  2.8 0.9 %copy-start.1 = (bf16[32,1536]{1,0:T(8,128)(2,1)S(1)}, bf16[32,1536]{1,0:T(8,128)(2,1)}, u32[]{:S(2)}) copy-start(bf16[32,1536]{1,0:T(8,128)(2,1)} %h_ref.1) | copy-start | bytes 294916

commit v2 on v1

--- a/solution.py
+++ b/solution.py
@@ -74,21 +74,21 @@
 
 
 def pair_matrix(ids, gates, q, n_e, cap, scale):
-    toks, topk = ids.shape
-    lane = lax.broadcasted_iota(jnp.int32, (toks, LANES), 1)
-    lane_e, lane_q, lane_c = lane // (n_e * cap), (lane // cap) % n_e, lane % cap
-    named = jnp.zeros((toks, LANES), jnp.float32)
-    gate = jnp.zeros((toks, LANES), jnp.float32)
+    topk, toks = ids.shape
+    slot = lax.broadcasted_iota(jnp.int32, (LANES, toks), 0)
+    slot_e, slot_q, slot_c = slot // (n_e * cap), (slot // cap) % n_e, slot % cap
+    named = jnp.zeros((LANES, toks), jnp.float32)
+    gate = jnp.zeros((LANES, toks), jnp.float32)
     for k in range(topk):
-        same = ids[:, k : k + 1] == lane_e
+        same = ids[k : k + 1, :] == slot_e
         named = named + jnp.where(same, 1.0, 0.0)
-        gate = gate + jnp.where(same, gates[:, k : k + 1], 0.0)
+        gate = gate + jnp.where(same, gates[k : k + 1, :], 0.0)
     row = lax.broadcasted_iota(jnp.int32, (toks, toks), 0)
     col = lax.broadcasted_iota(jnp.int32, (toks, toks), 1)
-    earlier = jnp.where(col < row, 1.0, 0.0).astype(jnp.bfloat16)
-    position = jnp.dot(earlier, named.astype(jnp.bfloat16), preferred_element_type=jnp.float32)
-    held = (position == lane_c.astype(jnp.float32)) & (lane_q == q)
-    slots = jnp.where(held, gate, 0.0).T
+    earlier = jnp.where(row < col, 1.0, 0.0).astype(jnp.bfloat16)
+    position = jnp.dot(named.astype(jnp.bfloat16), earlier, preferred_element_type=jnp.float32)
+    held = (position == slot_c.astype(jnp.float32)) & (slot_q == q)
+    slots = jnp.where(held, gate, 0.0)
     high = slots.astype(jnp.bfloat16)
     low = (slots - high.astype(jnp.float32)).astype(jnp.bfloat16)
     nt = (((1,), (1,)), ((), ()))
@@ -101,9 +101,9 @@
 def kernel(
     n_dp, n_e, cap, scale,
     h_ref, dir_ref, ids_ref, gates_ref,
-    adj_ref, hall,
-    dirv, tang, pairs, wf, wall,
-    loc_sem, own_send, relay_send, hz_recv, hs_send, hs_recv,
+    adj_out, hall_out,
+    adj, hall, dirv, idv, gatev, tang, pairs, wf, wall,
+    loc_sem, out_sem, own_send, relay_send, hz_recv, hs_send, hs_recv,
     a_send, a_recv, w_send, w_recv, ws_send, ws_recv, t_send, t_recv,
 ):
     n_z = n_dp // CORES
@@ -118,8 +118,12 @@
 
     load_dir = pltpu.make_async_copy(dir_ref.at[0], dirv, loc_sem.at[0])
     load_h = pltpu.make_async_copy(h_ref, hall.at[p], loc_sem.at[1])
+    load_ids = pltpu.make_async_copy(ids_ref, idv, loc_sem.at[2])
+    load_gates = pltpu.make_async_copy(gates_ref, gatev, loc_sem.at[3])
+    load_ids.start()
+    load_gates.start()
+    load_h.start()
     load_dir.start()
-    load_h.start()
 
     def z_peer(d):
         return lax.rem(z + d, n_z)
@@ -133,6 +137,10 @@
     for d in range(1, n_e):
         pl.semaphore_signal(barrier, inc=1, device_id=(p, e_peer(d)), device_id_type=MESH)
     pl.semaphore_signal(barrier, inc=1, device_id=(sib, e), device_id_type=MESH)
+    mine = pl.ds(pl.multiple_of(e * rows, rows), rows)
+    tang[:, mine, feat // LANES * LANES :] = jnp.zeros(
+        (n_dp, rows, tang.shape[2] - feat // LANES * LANES), jnp.bfloat16
+    )
     pl.semaphore_wait(barrier, n_z + n_e - 1)
 
     def remote(src, dst, send, recv, dev):
@@ -160,7 +168,9 @@
 
     sibling_copy(z, h_ref).start()
 
-    pairs[...] = pair_matrix(ids_ref[...], gates_ref[...], e, n_e, cap, scale)
+    load_ids.wait()
+    load_gates.wait()
+    pairs[...] = pair_matrix(idv[...], gatev[...], e, n_e, cap, scale)
 
     def slot_rows(owner, source):
         return pl.ds(pl.multiple_of(owner * rows + source * cap, cap), cap)
@@ -176,16 +186,16 @@
         pair_copy(d).start()
     wf[pl.ds(pl.multiple_of(e * cap, cap), cap), :] = pairs[slot_rows(e, e), :]
 
-    mine = pl.ds(pl.multiple_of(e * rows, rows), rows)
-    tang[:, mine, feat // LANES * LANES :] = jnp.zeros(
-        (n_dp, rows, tang.shape[2] - feat // LANES * LANES), jnp.bfloat16
-    )
-
     def tangent_copy(zs, d):
         ref = tang.at[pl.ds(zs * CORES, CORES), mine]
         return remote(ref, ref, t_send.at[zs, d], t_recv.at[zs, e], (p, e_peer(d)))
 
+    def rows_out(zs):
+        two = pl.ds(zs * CORES, CORES)
+        return pltpu.make_async_copy(hall.at[two], hall_out.at[two], out_sem.at[0, zs])
+
     def tangents(zs):
+        rows_out(zs).start()
         block = hall[pl.ds(zs * CORES, CORES)].reshape(CORES * rows, hall.shape[2])
         out = lax.dot_general(block, dirv[...], nt, preferred_element_type=jnp.float32)
         tang[pl.ds(zs * CORES, CORES), mine, :feat] = out.astype(jnp.bfloat16).reshape(CORES, rows, feat)
@@ -197,16 +207,6 @@
     sibling_copy(z, h_ref).wait_recv()
     tangents(z)
 
-    for d in range(1, n_e):
-        src = e_peer(d)
-        remote(
-            pairs.at[slot_rows(e, src)], wf.at[pl.ds(pl.multiple_of(src * cap, cap), cap)],
-            a_send.at[d], a_recv.at[src], (p, src),
-        ).wait_recv()
-    weights = wf[...]
-    high = weights.astype(jnp.bfloat16).astype(jnp.float32)
-    wall[p] = (high + swap_blocks(weights - high, cap)).astype(jnp.bfloat16)
-
     def weight_copy(d):
         return remote(wall.at[p], wall.at[p], w_send.at[d], w_recv.at[z], (z_peer(d) * CORES + core, e))
 
@@ -214,9 +214,24 @@
         ref = wall.at[zs * CORES + core]
         return remote(ref, ref, ws_send.at[zs], ws_recv.at[zs], (sib, e))
 
-    for d in range(1, n_z):
-        weight_copy(d).start()
-    weight_sibling(z).start()
+    def share_weights():
+        for d in range(1, n_e):
+            src = e_peer(d)
+            remote(
+                pairs.at[slot_rows(e, src)], wf.at[pl.ds(pl.multiple_of(src * cap, cap), cap)],
+                a_send.at[d], a_recv.at[src], (p, src),
+            ).wait_recv()
+        weights = wf[...]
+        high = weights.astype(jnp.bfloat16).astype(jnp.float32)
+        wall[p] = (high + swap_blocks(weights - high, cap)).astype(jnp.bfloat16)
+        for d in range(1, n_z):
+            weight_copy(d).start()
+        weight_sibling(z).start()
+
+    def forward_weights(zs):
+        ref = wall.at[zs * CORES + core]
+        remote(ref, ref, w_send.at[1], w_recv.at[zs], (sib, e)).wait_recv()
+        weight_sibling(zs).start()
 
     near = jnp.minimum(z, n_z - 1 - z)
 
@@ -240,6 +255,10 @@
     lane = lax.broadcasted_iota(jnp.int32, (rows, LANES), 1)
     row = lax.broadcasted_iota(jnp.int32, (rows, LANES), 0)
     direct = (lane // cap) % n_e == row // cap
+
+    def adjoint_out(zs):
+        two = pl.ds(zs * CORES, CORES)
+        return pltpu.make_async_copy(adj.at[two], adj_out.at[two], out_sem.at[1, zs])
 
     def finish(zs):
         weight_sibling(zs).wait_recv()
@@ -254,7 +273,8 @@
             both = jnp.concatenate([high, low], axis=0).astype(jnp.bfloat16)
             out = jnp.dot(both, tang[zs * CORES + k], preferred_element_type=jnp.float32)
             out = (out[:rows] + out[rows:]).astype(jnp.bfloat16)
-            adj_ref[zs * CORES + k] = out[:, :feat]
+            adj[zs * CORES + k] = out[:, :feat]
+        adjoint_out(zs).start()
 
     for j in range(1, n_z):
         zs = source(j)
@@ -262,13 +282,15 @@
             relay_copy(zs, c).wait_recv()
             relays(zs, lambda zs=zs, c=c: relay_copy(zs, c).start())
         sibling_copy(zs, hall.at[zs * CORES + core]).start()
+        if j == 1:
+            share_weights()
         sibling_copy(zs, hall.at[zs * CORES + core]).wait_recv()
         tangents(zs)
-        remote(
-            wall.at[zs * CORES + core], wall.at[zs * CORES + core], w_send.at[1], w_recv.at[zs], (sib, e)
-        ).wait_recv()
-        weight_sibling(zs).start()
-        finish(source(j - 1))
+        if j >= 2:
+            forward_weights(source(j - 1))
+            finish(source(j - 2))
+    forward_weights(source(n_z - 1))
+    finish(source(n_z - 2))
     finish(source(n_z - 1))
 
     for c in range(CHUNKS):
@@ -280,6 +302,8 @@
         weight_copy(d).wait_send()
     for j in range(n_z):
         zs = source(j)
+        adjoint_out(zs).wait()
+        rows_out(zs).wait()
         sibling_copy(zs, hall.at[zs * CORES + core]).wait_send()
         weight_sibling(zs).wait_send()
         for d in range(1, n_e):
@@ -299,8 +323,7 @@
     n_z = n_dp // CORES
     wide = -(-feat // LANES) * LANES
     scale = 1.0 / math.sqrt(expert_ids.shape[0] * n_dp * n_e)
-    vmem = pl.BlockSpec(memory_space=pltpu.VMEM)
-    hbm = pl.BlockSpec(memory_space=pl.ANY)
+    hbm = pl.BlockSpec(memory_space=pltpu.HBM)
     dma = pltpu.SemaphoreType.DMA
     adjoint, rows_all = pl.pallas_call(
         functools.partial(kernel, n_dp, n_e, cap, scale),
@@ -308,15 +331,20 @@
             jax.ShapeDtypeStruct((n_dp, rows, feat), jnp.bfloat16),
             jax.ShapeDtypeStruct((n_dp, rows, fw), jnp.bfloat16),
         ),
-        in_specs=[hbm, hbm, vmem, vmem],
-        out_specs=(vmem, vmem),
+        in_specs=[hbm] * 4,
+        out_specs=(hbm, hbm),
         scratch_shapes=[
+            pltpu.VMEM((n_dp, rows, feat), jnp.bfloat16),
+            pltpu.VMEM((n_dp, rows, fw), jnp.bfloat16),
             pltpu.VMEM((feat, fw), jnp.bfloat16),
+            pltpu.VMEM(expert_ids.shape[::-1], jnp.int32),
+            pltpu.VMEM(gate_weights.shape[::-1], jnp.float32),
             pltpu.VMEM((n_dp, n_e * rows, wide), jnp.bfloat16),
             pltpu.VMEM((LANES, LANES), jnp.float32),
             pltpu.VMEM((rows, LANES), jnp.float32),
             pltpu.VMEM((n_dp, rows, LANES), jnp.bfloat16),
-            dma((2,)),
+            dma((4,)),
+            dma((2, n_z)),
             dma((2, CHUNKS)),
             dma((n_z, CHUNKS)),
             dma((n_z, CHUNKS)),
@@ -332,9 +360,9 @@
             dma((n_z, n_e)),
         ],
         compiler_params=pltpu.CompilerParams(
-            collective_id=0, has_side_effects=True, vmem_limit_bytes=32 * 1024 * 1024
+            collective_id=0, has_side_effects=True, vmem_limit_bytes=56 * 1024 * 1024
         ),
-    )(cached_hidden, direction, expert_ids, gate_weights)
+    )(cached_hidden, direction, expert_ids.T, gate_weights.T)
     gradient = lax.dot_general(
         adjoint.reshape(n_dp * rows, feat),
         rows_all.reshape(n_dp * rows, fw),

time: 32.1 us -> 28.3 us (0.88)
  local copies, waits for them, and re-layouts: 3.71 us -> 0 us
  matrix products: 1.83 us -> 3.07 us
  Pallas kernels: 26.3 us -> 25.1 us
    unnamed x6 -> x0, local copies, waits for them, and re-layouts: 3.71 us -> none
    pallas_call x1, Pallas kernels: 26.3 us -> 25.1 us  [body(): pl.pallas_call(functools.partial(kernel, n_dp, n_e, cap, scale), out_shap...]
    dot_general x1, matrix products: 1.83 us -> 3.07 us  [body(): lax.dot_general(adjoint.reshape(n_dp * rows, feat), rows_all.reshape(n_dp...]
where the time goes in v2:
time: 28.3 us; the launch traced here: 28.1 us
  Pallas kernels  25.1 us (89%)
  matrix products  3.07 us (11%)
    pallas_call x1, Pallas kernels, body(): pl.pallas_call(functools.partial(kernel, n_dp, n_e, cap, scale), out_shap...  25.1 us
    dot_general x1, matrix products, body(): lax.dot_general(adjoint.reshape(n_dp * rows, feat), rows_all.reshape(n_dp...  3.07 us

profile of v2, /device:TPU:0, one launch (start us, length us, event | category | flops | bytes accessed | tf_op | source)
XLA Modules:
  0.0 28.1 jit_solution(6739445234228774887)
XLA Ops:
  0.0 25.1 %shard_map.46 = (bf16[8,32,360]{2,1,0:T(8,128)(2,1)}, bf16[8,32,1536]{2,1,0:T(8,128)(2,1)}) custom-call(bf16[32,1536]{1,0:T(8,128)(2,1)} %h_ref.1, bf16[1,360,1536]{2,1,0:T(8,128)(2,1)} %dir_ref.1, s32[4,128]{1,0:T(4,128)} %bitcast.7, f32[4,128]{1,0:T(4,128)} %bitcast.8), custom_call_target="tpu_custom_call" | custom-call | tf_op jit(solution)/shard_map/pallas_call | solution.py:328
  25.1 3.1 %convolution_bitcast_fusion = f32[1,360,1536]{2,1,0:T(8,128)} fusion(bf16[8,32,360]{2,1,0:T(8,128)(2,1)} %get-tuple-element.7, bf16[8,32,1536]{2,1,0:T(8,128)(2,1)} %get-tuple-element.8), kind=kOutput, calls=%fused_computation | convolution fusion | flops 283115520 | bytes 3182592 | tf_op jit(solution)/shard_map/dot_general | solution.py:366

commit v3 on v2

--- a/solution.py
+++ b/solution.py
@@ -103,7 +103,7 @@
     h_ref, dir_ref, ids_ref, gates_ref,
     adj_out, hall_out,
     adj, hall, dirv, idv, gatev, tang, pairs, wf, wall,
-    loc_sem, out_sem, own_send, relay_send, hz_recv, hs_send, hs_recv,
+    loc_sem, out_sem, own_send, far_send, relay_send, hz_recv, hs_send, hs_recv,
     a_send, a_recv, w_send, w_recv, ws_send, ws_recv, t_send, t_recv,
 ):
     n_z = n_dp // CORES
@@ -162,6 +162,22 @@
         for side in range(2):
             on_side(side, lambda side=side, c=c: own_copy(side, c).start())
 
+    at_end = (z == 0) | (z == n_z - 1)
+
+    def far_copy(d, c):
+        to = jnp.where(z == 0, d, n_z - 1 - d)
+        return remote(
+            h_ref.at[pl.ds(c * part, part)], hall.at[p, pl.ds(c * part, part)],
+            far_send.at[d, c], hz_recv.at[z, c], (to * CORES + core, e),
+        )
+
+    def far(d, act):
+        def both():
+            for c in range(CHUNKS):
+                act(far_copy(d, c))
+
+        pl.when(at_end)(both)
+
     def sibling_copy(zs, src):
         row = zs * CORES + core
         return remote(src, hall.at[row], hs_send.at[zs], hs_recv.at[zs], (sib, e))
@@ -184,6 +200,7 @@
 
     for d in range(1, n_e):
         pair_copy(d).start()
+    far(2, lambda copy: copy.start())
     wf[pl.ds(pl.multiple_of(e * cap, cap), cap), :] = pairs[slot_rows(e, e), :]
 
     def tangent_copy(zs, d):
@@ -250,7 +267,7 @@
 
     def relays(zs, fn):
         to = jnp.where(zs < z, z + 1, z - 1)
-        pl.when((to >= 0) & (to < n_z))(fn)
+        pl.when((to >= 0) & (to < n_z) & (zs > 0) & (zs < n_z - 1))(fn)
 
     lane = lax.broadcasted_iota(jnp.int32, (rows, LANES), 1)
     row = lax.broadcasted_iota(jnp.int32, (rows, LANES), 0)
@@ -282,6 +299,8 @@
             relay_copy(zs, c).wait_recv()
             relays(zs, lambda zs=zs, c=c: relay_copy(zs, c).start())
         sibling_copy(zs, hall.at[zs * CORES + core]).start()
+        if j + 2 < n_z:
+            far(j + 2, lambda copy: copy.start())
         if j == 1:
             share_weights()
         sibling_copy(zs, hall.at[zs * CORES + core]).wait_recv()
@@ -296,6 +315,8 @@
     for c in range(CHUNKS):
         for side in range(2):
             on_side(side, lambda side=side, c=c: own_copy(side, c).wait_send())
+    for d in range(2, n_z):
+        far(d, lambda copy: copy.wait_send())
     for d in range(1, n_e):
         pair_copy(d).wait_send()
     for d in range(1, n_z):
@@ -318,7 +339,7 @@
     rows, fw = cached_hidden.shape
     cap = rows // n_e
     feat = direction.shape[1]
-    if n_e * rows != LANES or cap % 8 or rows % (16 * CHUNKS) or n_dp % CORES or n_dp < 2 * CORES:
+    if n_e * rows != LANES or cap % 8 or rows % (16 * CHUNKS) or n_dp % CORES or n_dp < 3 * CORES:
         return general_body(cached_hidden, direction, expert_ids, gate_weights)
     n_z = n_dp // CORES
     wide = -(-feat // LANES) * LANES
@@ -348,6 +369,7 @@
             dma((2, CHUNKS)),
             dma((n_z, CHUNKS)),
             dma((n_z, CHUNKS)),
+            dma((n_z, CHUNKS)),
             dma((n_z,)),
             dma((n_z,)),
             dma((n_e,)),

time: 28.3 us -> 29.4 us (1.039)
  Pallas kernels: 25.1 us -> 26.1 us
    pallas_call x1, Pallas kernels: 25.1 us -> 26.1 us  [body(): pl.pallas_call(functools.partial(kernel, n_dp, n_e, cap, scale), out_shap...]
where the time goes in v3:
time: 29.4 us; the launch traced here: 29.2 us
  Pallas kernels  26.1 us (89%)
  matrix products  3.07 us (10%)
    pallas_call x1, Pallas kernels, body(): pl.pallas_call(functools.partial(kernel, n_dp, n_e, cap, scale), out_shap...  26.1 us
    dot_general x1, matrix products, body(): lax.dot_general(adjoint.reshape(n_dp * rows, feat), rows_all.reshape(n_dp...  3.07 us

profile of v3, /device:TPU:0, one launch (start us, length us, event | category | flops | bytes accessed | tf_op | source)
XLA Modules:
  0.0 29.2 jit_solution(1693830127195053174)
XLA Ops:
  0.0 26.1 %shard_map.46 = (bf16[8,32,360]{2,1,0:T(8,128)(2,1)}, bf16[8,32,1536]{2,1,0:T(8,128)(2,1)}) custom-call(bf16[32,1536]{1,0:T(8,128)(2,1)} %h_ref.1, bf16[1,360,1536]{2,1,0:T(8,128)(2,1)} %dir_ref.1, s32[4,128]{1,0:T(4,128)} %bitcast.7, f32[4,128]{1,0:T(4,128)} %bitcast.8), custom_call_target="tpu_custom_call" | custom-call | tf_op jit(solution)/shard_map/pallas_call | solution.py:349
  26.1 3.1 %convolution_bitcast_fusion = f32[1,360,1536]{2,1,0:T(8,128)} fusion(bf16[8,32,360]{2,1,0:T(8,128)(2,1)} %get-tuple-element.7, bf16[8,32,1536]{2,1,0:T(8,128)(2,1)} %get-tuple-element.8), kind=kOutput, calls=%fused_computation | convolution fusion | flops 283115520 | bytes 3182592 | tf_op jit(solution)/shard_map/dot_general | solution.py:388

commit v4 on v2

--- a/solution.py
+++ b/solution.py
@@ -104,7 +104,7 @@
     adj_out, hall_out,
     adj, hall, dirv, idv, gatev, tang, pairs, wf, wall,
     loc_sem, out_sem, own_send, relay_send, hz_recv, hs_send, hs_recv,
-    a_send, a_recv, w_send, w_recv, ws_send, ws_recv, t_send, t_recv,
+    a_send, a_recv, w_send, w_recv, ws_send, ws_recv, t_send, t_recv, o_send, o_recv,
 ):
     n_z = n_dp // CORES
     rows = n_e * cap
@@ -186,9 +186,32 @@
         pair_copy(d).start()
     wf[pl.ds(pl.multiple_of(e * cap, cap), cap), :] = pairs[slot_rows(e, e), :]
 
-    def tangent_copy(zs, d):
+    sides = (e + 1 - 2 * (e % 2), lax.rem(e + 2, n_e))
+    across = n_e - 1 - e
+
+    def expert_rows(owner):
+        return pl.ds(pl.multiple_of(owner * rows, rows), rows)
+
+    def tangent_copy(zs, i):
         ref = tang.at[pl.ds(zs * CORES, CORES), mine]
-        return remote(ref, ref, t_send.at[zs, d], t_recv.at[zs, e], (p, e_peer(d)))
+        return remote(ref, ref, t_send.at[zs, i], t_recv.at[zs, i], (p, sides[i]))
+
+    def tangent_arrival(zs, i):
+        ref = tang.at[pl.ds(zs * CORES, CORES), expert_rows(sides[i])]
+        return remote(ref, ref, t_send.at[zs, i], t_recv.at[zs, i], (p, sides[i]))
+
+    def onward_copy(zs, i):
+        ref = tang.at[zs * CORES + i, expert_rows(sides[i])]
+        return remote(ref, ref, o_send.at[zs, i], o_recv.at[zs, i], (p, sides[1 - i]))
+
+    def onward_arrival(zs, i):
+        ref = tang.at[zs * CORES + i, expert_rows(across)]
+        return remote(ref, ref, o_send.at[zs, i], o_recv.at[zs, i], (p, sides[1 - i]))
+
+    def pass_on(zs):
+        for i in range(2):
+            tangent_arrival(zs, i).wait_recv()
+            onward_copy(zs, i).start()
 
     def rows_out(zs):
         two = pl.ds(zs * CORES, CORES)
@@ -199,8 +222,8 @@
         block = hall[pl.ds(zs * CORES, CORES)].reshape(CORES * rows, hall.shape[2])
         out = lax.dot_general(block, dirv[...], nt, preferred_element_type=jnp.float32)
         tang[pl.ds(zs * CORES, CORES), mine, :feat] = out.astype(jnp.bfloat16).reshape(CORES, rows, feat)
-        for d in range(1, n_e):
-            tangent_copy(zs, d).start()
+        for i in range(2):
+            tangent_copy(zs, i).start()
 
     load_dir.wait()
     load_h.wait()
@@ -262,10 +285,8 @@
 
     def finish(zs):
         weight_sibling(zs).wait_recv()
-        for d in range(1, n_e):
-            src = e_peer(d)
-            ref = tang.at[pl.ds(zs * CORES, CORES), pl.ds(pl.multiple_of(src * rows, rows), rows)]
-            remote(ref, ref, t_send.at[zs, d], t_recv.at[zs, src], (p, src)).wait_recv()
+        for i in range(2):
+            onward_arrival(zs, i).wait_recv()
         for k in range(CORES):
             packed = wall[zs * CORES + k].astype(jnp.float32)
             high = jnp.where(direct, packed, 0.0)
@@ -286,11 +307,13 @@
             share_weights()
         sibling_copy(zs, hall.at[zs * CORES + core]).wait_recv()
         tangents(zs)
+        pass_on(source(j - 1))
         if j >= 2:
             forward_weights(source(j - 1))
             finish(source(j - 2))
     forward_weights(source(n_z - 1))
     finish(source(n_z - 2))
+    pass_on(source(n_z - 1))
     finish(source(n_z - 1))
 
     for c in range(CHUNKS):
@@ -306,11 +329,20 @@
         rows_out(zs).wait()
         sibling_copy(zs, hall.at[zs * CORES + core]).wait_send()
         weight_sibling(zs).wait_send()
-        for d in range(1, n_e):
-            tangent_copy(zs, d).wait_send()
+        for i in range(2):
+            tangent_copy(zs, i).wait_send()
+            onward_copy(zs, i).wait_send()
         if j:
             for c in range(CHUNKS):
                 relays(zs, lambda zs=zs, c=c: relay_copy(zs, c).wait_send())
+
+
+def outer_kernel(adj_ref, rows_ref, out_ref, turned):
+    @pl.when(pl.program_id(0) == 0)
+    def _():
+        turned[...] = adj_ref[...].T
+
+    out_ref[0] = jnp.dot(turned[...], rows_ref[...], preferred_element_type=jnp.float32)
 
 
 def body(cached_hidden, direction, expert_ids, gate_weights):
@@ -318,7 +350,7 @@
     rows, fw = cached_hidden.shape
     cap = rows // n_e
     feat = direction.shape[1]
-    if n_e * rows != LANES or cap % 8 or rows % (16 * CHUNKS) or n_dp % CORES or n_dp < 2 * CORES:
+    if n_e != 4 or n_e * rows != LANES or cap % 8 or rows % (16 * CHUNKS) or n_dp % CORES or n_dp < 2 * CORES:
         return general_body(cached_hidden, direction, expert_ids, gate_weights)
     n_z = n_dp // CORES
     wide = -(-feat // LANES) * LANES
@@ -356,20 +388,27 @@
             dma((n_z,)),
             dma((n_z,)),
             dma((n_z,)),
-            dma((n_z, n_e)),
-            dma((n_z, n_e)),
+            dma((n_z, 2)),
+            dma((n_z, 2)),
+            dma((n_z, 2)),
+            dma((n_z, 2)),
         ],
         compiler_params=pltpu.CompilerParams(
             collective_id=0, has_side_effects=True, vmem_limit_bytes=56 * 1024 * 1024
         ),
     )(cached_hidden, direction, expert_ids.T, gate_weights.T)
-    gradient = lax.dot_general(
-        adjoint.reshape(n_dp * rows, feat),
-        rows_all.reshape(n_dp * rows, fw),
-        (((0,), (0,)), ((), ())),
-        preferred_element_type=jnp.float32,
-    )
-    return gradient.reshape(1, feat, fw)
+    tile = fw // 3 if fw % (3 * LANES) == 0 else fw
+    return pl.pallas_call(
+        outer_kernel,
+        grid=(fw // tile,),
+        out_shape=jax.ShapeDtypeStruct((1, feat, fw), jnp.float32),
+        in_specs=[
+            pl.BlockSpec((n_dp * rows, feat), lambda i: (0, 0)),
+            pl.BlockSpec((n_dp * rows, tile), lambda i: (0, i)),
+        ],
+        out_specs=pl.BlockSpec((1, feat, tile), lambda i: (0, 0, i)),
+        scratch_shapes=[pltpu.VMEM((feat, n_dp * rows), jnp.bfloat16)],
+    )(adjoint.reshape(n_dp * rows, feat), rows_all.reshape(n_dp * rows, fw))
 
 
 def solution(mesh):

time: 28.3 us -> 32.4 us (1.14)
  Pallas kernels: 25.1 us -> 32.2 us
  matrix products: 3.07 us -> 0 us
    pallas_call x0 -> x1, Pallas kernels: none -> 3.64 us  [body(): pl.pallas_call(outer_kernel, grid=(fw // tile,), out_shape=jax.ShapeDtype...]
    pallas_call x1, Pallas kernels: 25.1 us -> 28.5 us  [body(): pl.pallas_call(functools.partial(kernel, n_dp, n_e, cap, scale), out_shap...]
    dot_general x1 -> x0, matrix products: 3.07 us -> none  [body(): lax.dot_general(adjoint.reshape(n_dp * rows, feat), rows_all.reshape(n_dp...]
where the time goes in v4:
time: 32.4 us; the launch traced here: 32.2 us
  Pallas kernels  32.2 us (99%)
    pallas_call x1, Pallas kernels, body(): pl.pallas_call(functools.partial(kernel, n_dp, n_e, cap, scale), out_shap...  28.5 us
    pallas_call x1, Pallas kernels, body(): pl.pallas_call(outer_kernel, grid=(fw // tile,), out_shape=jax.ShapeDtype...  3.64 us

profile of v4, /device:TPU:0, one launch (start us, length us, event | category | flops | bytes accessed | tf_op | source)
XLA Modules:
  0.0 32.2 jit_solution(9586659259842027093)
XLA Ops:
  0.0 28.5 %shard_map.46 = (bf16[8,32,360]{2,1,0:T(8,128)(2,1)}, bf16[8,32,1536]{2,1,0:T(8,128)(2,1)}) custom-call(bf16[32,1536]{1,0:T(8,128)(2,1)} %h_ref.1, bf16[1,360,1536]{2,1,0:T(8,128)(2,1)} %dir_ref.1, s32[4,128]{1,0:T(4,128)} %bitcast.6, f32[4,128]{1,0:T(4,128)} %bitcast.7), custom_call_target="tpu_custom_call" | custom-call | tf_op jit(solution)/shard_map/pallas_call | solution.py:360
  28.6 3.6 %shard_map.47 = f32[1,360,1536]{2,1,0:T(8,128)} custom-call(bf16[256,360]{1,0:T(8,128)(2,1)} %bitcast.5, bf16[256,1536]{1,0:T(8,128)(2,1)} %bitcast.4), custom_call_target="tpu_custom_call" | custom-call | tf_op jit(solution)/shard_map/pallas_call | solution.py:401

commit v5 on v2

--- a/solution.py
+++ b/solution.py
@@ -102,7 +102,7 @@
     n_dp, n_e, cap, scale,
     h_ref, dir_ref, ids_ref, gates_ref,
     adj_out, hall_out,
-    adj, hall, dirv, idv, gatev, tang, pairs, wf, wall,
+    adj, hall, dirv, dirt, idv, gatev, tang, pairs, wf, wall,
     loc_sem, out_sem, own_send, relay_send, hz_recv, hs_send, hs_recv,
     a_send, a_recv, w_send, w_recv, ws_send, ws_recv, t_send, t_recv,
 ):
@@ -114,7 +114,6 @@
     e = lax.axis_index("expert")
     z, core = p // CORES, p % CORES
     sib = z * CORES + (1 - core)
-    nt = (((1,), (1,)), ((), ()))
 
     load_dir = pltpu.make_async_copy(dir_ref.at[0], dirv, loc_sem.at[0])
     load_h = pltpu.make_async_copy(h_ref, hall.at[p], loc_sem.at[1])
@@ -191,18 +190,20 @@
         return remote(ref, ref, t_send.at[zs, d], t_recv.at[zs, e], (p, e_peer(d)))
 
     def rows_out(zs):
-        two = pl.ds(zs * CORES, CORES)
-        return pltpu.make_async_copy(hall.at[two], hall_out.at[two], out_sem.at[0, zs])
+        two = pl.ds(pl.multiple_of(zs * CORES * rows, CORES * rows), CORES * rows)
+        src = hall.reshape(n_dp * rows, hall.shape[2])
+        return pltpu.make_async_copy(src.at[two], hall_out.at[two], out_sem.at[0, zs])
 
     def tangents(zs):
         rows_out(zs).start()
         block = hall[pl.ds(zs * CORES, CORES)].reshape(CORES * rows, hall.shape[2])
-        out = lax.dot_general(block, dirv[...], nt, preferred_element_type=jnp.float32)
+        out = jnp.dot(block, dirt[...], preferred_element_type=jnp.float32)
         tang[pl.ds(zs * CORES, CORES), mine, :feat] = out.astype(jnp.bfloat16).reshape(CORES, rows, feat)
         for d in range(1, n_e):
             tangent_copy(zs, d).start()
 
     load_dir.wait()
+    dirt[...] = dirv[...].T
     load_h.wait()
     sibling_copy(z, h_ref).wait_recv()
     tangents(z)
@@ -257,7 +258,7 @@
     direct = (lane // cap) % n_e == row // cap
 
     def adjoint_out(zs):
-        two = pl.ds(zs * CORES, CORES)
+        two = pl.ds(pl.multiple_of(zs * CORES * rows, CORES * rows), CORES * rows)
         return pltpu.make_async_copy(adj.at[two], adj_out.at[two], out_sem.at[1, zs])
 
     def finish(zs):
@@ -273,7 +274,7 @@
             both = jnp.concatenate([high, low], axis=0).astype(jnp.bfloat16)
             out = jnp.dot(both, tang[zs * CORES + k], preferred_element_type=jnp.float32)
             out = (out[:rows] + out[rows:]).astype(jnp.bfloat16)
-            adj[zs * CORES + k] = out[:, :feat]
+            adj[pl.ds(pl.multiple_of((zs * CORES + k) * rows, rows), rows), :] = out[:, :feat]
         adjoint_out(zs).start()
 
     for j in range(1, n_z):
@@ -284,11 +285,11 @@
         sibling_copy(zs, hall.at[zs * CORES + core]).start()
         if j == 1:
             share_weights()
-        sibling_copy(zs, hall.at[zs * CORES + core]).wait_recv()
-        tangents(zs)
         if j >= 2:
             forward_weights(source(j - 1))
             finish(source(j - 2))
+        sibling_copy(zs, hall.at[zs * CORES + core]).wait_recv()
+        tangents(zs)
     forward_weights(source(n_z - 1))
     finish(source(n_z - 2))
     finish(source(n_z - 1))
@@ -328,15 +329,16 @@
     adjoint, rows_all = pl.pallas_call(
         functools.partial(kernel, n_dp, n_e, cap, scale),
         out_shape=(
-            jax.ShapeDtypeStruct((n_dp, rows, feat), jnp.bfloat16),
-            jax.ShapeDtypeStruct((n_dp, rows, fw), jnp.bfloat16),
+            jax.ShapeDtypeStruct((n_dp * rows, feat), jnp.bfloat16),
+            jax.ShapeDtypeStruct((n_dp * rows, fw), jnp.bfloat16),
         ),
         in_specs=[hbm] * 4,
         out_specs=(hbm, hbm),
         scratch_shapes=[
-            pltpu.VMEM((n_dp, rows, feat), jnp.bfloat16),
+            pltpu.VMEM((n_dp * rows, feat), jnp.bfloat16),
             pltpu.VMEM((n_dp, rows, fw), jnp.bfloat16),
             pltpu.VMEM((feat, fw), jnp.bfloat16),
+            pltpu.VMEM((fw, feat), jnp.bfloat16),
             pltpu.VMEM(expert_ids.shape[::-1], jnp.int32),
             pltpu.VMEM(gate_weights.shape[::-1], jnp.float32),
             pltpu.VMEM((n_dp, n_e * rows, wide), jnp.bfloat16),
@@ -364,8 +366,8 @@
         ),
     )(cached_hidden, direction, expert_ids.T, gate_weights.T)
     gradient = lax.dot_general(
-        adjoint.reshape(n_dp * rows, feat),
-        rows_all.reshape(n_dp * rows, fw),
+        adjoint,
+        rows_all,
         (((0,), (0,)), ((), ())),
         preferred_element_type=jnp.float32,
     )

time: 28.3 us -> 27.9 us (0.986)
  Pallas kernels: 25.1 us -> 24.7 us
    pallas_call x1, Pallas kernels: 25.1 us -> 24.7 us  [body(): pl.pallas_call(functools.partial(kernel, n_dp, n_e, cap, scale), out_shap...]
where the time goes in v5:
time: 27.9 us; the launch traced here: 27.7 us
  Pallas kernels  24.7 us (89%)
  matrix products  3.07 us (11%)
    pallas_call x1, Pallas kernels, body(): pl.pallas_call(functools.partial(kernel, n_dp, n_e, cap, scale), out_shap...  24.7 us
    dot_general x1, matrix products, body(): lax.dot_general(adjoint, rows_all, (((0,), (0,)), ((), ())), preferred_el...  3.07 us

profile of v5, /device:TPU:0, one launch (start us, length us, event | category | flops | bytes accessed | tf_op | source)
XLA Modules:
  0.0 27.7 jit_solution(4810644400616821447)
XLA Ops:
  0.0 24.7 %shard_map.46 = (bf16[256,360]{1,0:T(8,128)(2,1)}, bf16[256,1536]{1,0:T(8,128)(2,1)}) custom-call(bf16[32,1536]{1,0:T(8,128)(2,1)} %h_ref.1, bf16[1,360,1536]{2,1,0:T(8,128)(2,1)} %dir_ref.1, s32[4,128]{1,0:T(4,128)} %bitcast.6, f32[4,128]{1,0:T(4,128)} %bitcast.7), custom_call_target="tpu_custom_call" | custom-call | tf_op jit(solution)/shard_map/pallas_call | solution.py:329
  24.7 3.1 %convolution_bitcast_fusion = f32[1,360,1536]{2,1,0:T(8,128)} fusion(bf16[256,360]{1,0:T(8,128)(2,1)} %get-tuple-element.7, bf16[256,1536]{1,0:T(8,128)(2,1)} %get-tuple-element.8), kind=kOutput, calls=%fused_computation | convolution fusion | flops 283115520 | bytes 3182592 | tf_op jit(solution)/shard_map/dot_general | solution.py:368

commit v6 on v5

--- a/solution.py
+++ b/solution.py
@@ -104,7 +104,7 @@
     adj_out, hall_out,
     adj, hall, dirv, dirt, idv, gatev, tang, pairs, wf, wall,
     loc_sem, out_sem, own_send, relay_send, hz_recv, hs_send, hs_recv,
-    a_send, a_recv, w_send, w_recv, ws_send, ws_recv, t_send, t_recv,
+    a_send, a_recv, w_send, wr_send, w_recv, ws_send, ws_recv, t_send, t_recv,
 ):
     n_z = n_dp // CORES
     rows = n_e * cap
@@ -124,15 +124,19 @@
     load_h.start()
     load_dir.start()
 
-    def z_peer(d):
-        return lax.rem(z + d, n_z)
+    def on_side(side, fn):
+        pl.when(z + 1 < n_z if side == 0 else z > 0)(fn)
 
     def e_peer(d):
         return lax.rem(e + d, n_e)
 
     barrier = pltpu.get_barrier_semaphore()
-    for d in range(1, n_z):
-        pl.semaphore_signal(barrier, inc=1, device_id=(z_peer(d) * CORES + core, e), device_id_type=MESH)
+    for side in range(2):
+        to = (z + 1 if side == 0 else z - 1) * CORES + core
+        on_side(
+            side,
+            lambda to=to: pl.semaphore_signal(barrier, inc=1, device_id=(to, e), device_id_type=MESH),
+        )
     for d in range(1, n_e):
         pl.semaphore_signal(barrier, inc=1, device_id=(p, e_peer(d)), device_id_type=MESH)
     pl.semaphore_signal(barrier, inc=1, device_id=(sib, e), device_id_type=MESH)
@@ -140,7 +144,8 @@
     tang[:, mine, feat // LANES * LANES :] = jnp.zeros(
         (n_dp, rows, tang.shape[2] - feat // LANES * LANES), jnp.bfloat16
     )
-    pl.semaphore_wait(barrier, n_z + n_e - 1)
+    on_line = jnp.where(z > 0, 1, 0) + jnp.where(z + 1 < n_z, 1, 0)
+    pl.semaphore_wait(barrier, on_line + n_e)
 
     def remote(src, dst, send, recv, dev):
         return pltpu.make_async_remote_copy(
@@ -153,9 +158,6 @@
             h_ref.at[pl.ds(c * part, part)], hall.at[p, pl.ds(c * part, part)],
             own_send.at[side, c], hz_recv.at[z, c], (to * CORES + core, e),
         )
-
-    def on_side(side, fn):
-        pl.when(z + 1 < n_z if side == 0 else z > 0)(fn)
 
     for c in range(CHUNKS):
         for side in range(2):
@@ -208,8 +210,14 @@
     sibling_copy(z, h_ref).wait_recv()
     tangents(z)
 
-    def weight_copy(d):
-        return remote(wall.at[p], wall.at[p], w_send.at[d], w_recv.at[z], (z_peer(d) * CORES + core, e))
+    def weight_copy(side):
+        to = z + 1 if side == 0 else z - 1
+        return remote(wall.at[p], wall.at[p], w_send.at[side], w_recv.at[z], (to * CORES + core, e))
+
+    def weight_relay(zs):
+        to = jnp.where(zs < z, z + 1, z - 1)
+        ref = wall.at[zs * CORES + core]
+        return remote(ref, ref, wr_send.at[zs], w_recv.at[zs], (to * CORES + core, e))
 
     def weight_sibling(zs):
         ref = wall.at[zs * CORES + core]
@@ -225,13 +233,13 @@
         weights = wf[...]
         high = weights.astype(jnp.bfloat16).astype(jnp.float32)
         wall[p] = (high + swap_blocks(weights - high, cap)).astype(jnp.bfloat16)
-        for d in range(1, n_z):
-            weight_copy(d).start()
+        for side in range(2):
+            on_side(side, lambda side=side: weight_copy(side).start())
         weight_sibling(z).start()
 
     def forward_weights(zs):
-        ref = wall.at[zs * CORES + core]
-        remote(ref, ref, w_send.at[1], w_recv.at[zs], (sib, e)).wait_recv()
+        weight_relay(zs).wait_recv()
+        relays(zs, lambda: weight_relay(zs).start())
         weight_sibling(zs).start()
 
     near = jnp.minimum(z, n_z - 1 - z)
@@ -299,8 +307,8 @@
             on_side(side, lambda side=side, c=c: own_copy(side, c).wait_send())
     for d in range(1, n_e):
         pair_copy(d).wait_send()
-    for d in range(1, n_z):
-        weight_copy(d).wait_send()
+    for side in range(2):
+        on_side(side, lambda side=side: weight_copy(side).wait_send())
     for j in range(n_z):
         zs = source(j)
         adjoint_out(zs).wait()
@@ -312,6 +320,7 @@
         if j:
             for c in range(CHUNKS):
                 relays(zs, lambda zs=zs, c=c: relay_copy(zs, c).wait_send())
+            relays(zs, lambda zs=zs: weight_relay(zs).wait_send())
 
 
 def body(cached_hidden, direction, expert_ids, gate_weights):
@@ -354,6 +363,7 @@
             dma((n_z,)),
             dma((n_e,)),
             dma((n_e,)),
+            dma((2,)),
             dma((n_z,)),
             dma((n_z,)),
             dma((n_z,)),

time: 27.9 us -> 27.3 us (0.978)
  Pallas kernels: 24.7 us -> 24 us
    pallas_call x1, Pallas kernels: 24.7 us -> 24 us  [body(): pl.pallas_call(functools.partial(kernel, n_dp, n_e, cap, scale), out_shap...]
where the time goes in v6:
time: 27.3 us; the launch traced here: 27.1 us
  Pallas kernels  24 us (88%)
  matrix products  3.07 us (11%)
    pallas_call x1, Pallas kernels, body(): pl.pallas_call(functools.partial(kernel, n_dp, n_e, cap, scale), out_shap...  24 us
    dot_general x1, matrix products, body(): lax.dot_general(adjoint, rows_all, (((0,), (0,)), ((), ())), preferred_el...  3.07 us

profile of v6, /device:TPU:0, one launch (start us, length us, event | category | flops | bytes accessed | tf_op | source)
XLA Modules:
  0.0 27.1 jit_solution(3547382682498373577)
XLA Ops:
  0.0 24.0 %shard_map.46 = (bf16[256,360]{1,0:T(8,128)(2,1)}, bf16[256,1536]{1,0:T(8,128)(2,1)}) custom-call(bf16[32,1536]{1,0:T(8,128)(2,1)} %h_ref.1, bf16[1,360,1536]{2,1,0:T(8,128)(2,1)} %dir_ref.1, s32[4,128]{1,0:T(4,128)} %bitcast.6, f32[4,128]{1,0:T(4,128)} %bitcast.7), custom_call_target="tpu_custom_call" | custom-call | tf_op jit(solution)/shard_map/pallas_call | solution.py:338
  24.0 3.1 %convolution_bitcast_fusion = f32[1,360,1536]{2,1,0:T(8,128)} fusion(bf16[256,360]{1,0:T(8,128)(2,1)} %get-tuple-element.7, bf16[256,1536]{1,0:T(8,128)(2,1)} %get-tuple-element.8), kind=kOutput, calls=%fused_computation | convolution fusion | flops 283115520 | bytes 3182592 | tf_op jit(solution)/shard_map/dot_general | solution.py:378

commit v7 on v6

--- a/solution.py
+++ b/solution.py
@@ -248,7 +248,7 @@
         if j == 0:
             return z
         s = (j + 1) // 2
-        close = z - s if j % 2 else z + s
+        close = z + s if j % 2 else z - s
         far = jnp.where(2 * z < n_z - 1, j, n_z - 1 - j)
         return jnp.where(j <= 2 * near, close, far)
 
@@ -285,13 +285,20 @@
             adj[pl.ds(pl.multiple_of((zs * CORES + k) * rows, rows), rows), :] = out[:, :feat]
         adjoint_out(zs).start()
 
+    def take(zs):
+        for c in range(CHUNKS):
+            relay_copy(zs, c).wait_recv()
+            relays(zs, lambda c=c: relay_copy(zs, c).start())
+        sibling_copy(zs, hall.at[zs * CORES + core]).start()
+
     for j in range(1, n_z):
         zs = source(j)
-        for c in range(CHUNKS):
-            relay_copy(zs, c).wait_recv()
-            relays(zs, lambda zs=zs, c=c: relay_copy(zs, c).start())
-        sibling_copy(zs, hall.at[zs * CORES + core]).start()
+        if j == 2:
+            pl.when(near == 0)(lambda zs=zs: take(zs))
+        else:
+            take(zs)
         if j == 1:
+            pl.when(near > 0)(lambda: take(source(2)))
             share_weights()
         if j >= 2:
             forward_weights(source(j - 1))

time: 27.3 us -> 26.3 us (0.963)
  Pallas kernels: 24 us -> 23.1 us
    pallas_call x1, Pallas kernels: 24 us -> 23.1 us  [body(): pl.pallas_call(functools.partial(kernel, n_dp, n_e, cap, scale), out_shap...]
where the time goes in v7:
time: 26.3 us; the launch traced here: 26.2 us
  Pallas kernels  23.1 us (88%)
  matrix products  3.07 us (12%)
    pallas_call x1, Pallas kernels, body(): pl.pallas_call(functools.partial(kernel, n_dp, n_e, cap, scale), out_shap...  23.1 us
    dot_general x1, matrix products, body(): lax.dot_general(adjoint, rows_all, (((0,), (0,)), ((), ())), preferred_el...  3.07 us

profile of v7, /device:TPU:0, one launch (start us, length us, event | category | flops | bytes accessed | tf_op | source)
XLA Modules:
  0.0 26.2 jit_solution(5867917117456720427)
XLA Ops:
  0.0 23.1 %shard_map.46 = (bf16[256,360]{1,0:T(8,128)(2,1)}, bf16[256,1536]{1,0:T(8,128)(2,1)}) custom-call(bf16[32,1536]{1,0:T(8,128)(2,1)} %h_ref.1, bf16[1,360,1536]{2,1,0:T(8,128)(2,1)} %dir_ref.1, s32[4,128]{1,0:T(4,128)} %bitcast.6, f32[4,128]{1,0:T(4,128)} %bitcast.7), custom_call_target="tpu_custom_call" | custom-call | tf_op jit(solution)/shard_map/pallas_call | solution.py:345
  23.1 3.1 %convolution_bitcast_fusion = f32[1,360,1536]{2,1,0:T(8,128)} fusion(bf16[256,360]{1,0:T(8,128)(2,1)} %get-tuple-element.7, bf16[256,1536]{1,0:T(8,128)(2,1)} %get-tuple-element.8), kind=kOutput, calls=%fused_computation | convolution fusion | flops 283115520 | bytes 3182592 | tf_op jit(solution)/shard_map/dot_general | solution.py:385

commit v8 on v7

--- a/solution.py
+++ b/solution.py
@@ -160,7 +160,7 @@
         )
 
     for c in range(CHUNKS):
-        for side in range(2):
+        for side in (1, 0):
             on_side(side, lambda side=side, c=c: own_copy(side, c).start())
 
     def sibling_copy(zs, src):
@@ -293,8 +293,10 @@
 
     for j in range(1, n_z):
         zs = source(j)
-        if j == 2:
+        if j in (2, 3):
             pl.when(near == 0)(lambda zs=zs: take(zs))
+            if j == 2 and n_z > 3:
+                pl.when(near > 0)(lambda: take(source(3)))
         else:
             take(zs)
         if j == 1:

time: 26.3 us -> 25.1 us (0.954)
  Pallas kernels: 23.1 us -> 21.9 us
    pallas_call x1, Pallas kernels: 23.1 us -> 21.9 us  [body(): pl.pallas_call(functools.partial(kernel, n_dp, n_e, cap, scale), out_shap...]
where the time goes in v8:
time: 25.1 us; the launch traced here: 25 us
  Pallas kernels  21.9 us (87%)
  matrix products  3.07 us (12%)
    pallas_call x1, Pallas kernels, body(): pl.pallas_call(functools.partial(kernel, n_dp, n_e, cap, scale), out_shap...  21.9 us
    dot_general x1, matrix products, body(): lax.dot_general(adjoint, rows_all, (((0,), (0,)), ((), ())), preferred_el...  3.07 us

profile of v8, /device:TPU:0, one launch (start us, length us, event | category | flops | bytes accessed | tf_op | source)
XLA Modules:
  0.0 25.0 jit_solution(12867574769559080971)
XLA Ops:
  0.0 21.9 %shard_map.46 = (bf16[256,360]{1,0:T(8,128)(2,1)}, bf16[256,1536]{1,0:T(8,128)(2,1)}) custom-call(bf16[32,1536]{1,0:T(8,128)(2,1)} %h_ref.1, bf16[1,360,1536]{2,1,0:T(8,128)(2,1)} %dir_ref.1, s32[4,128]{1,0:T(4,128)} %bitcast.6, f32[4,128]{1,0:T(4,128)} %bitcast.7), custom_call_target="tpu_custom_call" | custom-call | tf_op jit(solution)/shard_map/pallas_call | solution.py:347
  21.9 3.1 %convolution_bitcast_fusion = f32[1,360,1536]{2,1,0:T(8,128)} fusion(bf16[256,360]{1,0:T(8,128)(2,1)} %get-tuple-element.7, bf16[256,1536]{1,0:T(8,128)(2,1)} %get-tuple-element.8), kind=kOutput, calls=%fused_computation | convolution fusion | flops 283115520 | bytes 3182592 | tf_op jit(solution)/shard_map/dot_general | solution.py:387
